TPU v7x, 128 devices: a whole 4x4x4 slice. The times are simulated.
128 devices in a mesh: prefix: 16 (over z, y), group: 8 (over x, core).
Axes of the slice: x: 4, y: 4, z: 4, core: 2. Of those that a mesh axis runs over, the one named last changes fastest.
Arguments:
- queries: bfloat16 [16, 256, 8192], P(None, 'group', 'prefix'), may hold values from -128 to 128
- cand_kv: bfloat16 [16, 256, 2048], P(None, 'group'), may hold values from -32 to 32
- prefix_kv: bfloat16 [16384, 2048], P('prefix'), may hold values from -32 to 32
- lengths: int32 [16], replicated, may hold values from 32 to 256, as said below
- owner: int32 [16], replicated, may hold values from 0 to 7, as said below
Outputs:
- scored: bfloat16 [16, 256, 8192], P('group', None, 'prefix')
Inputs may be any that keep to these rules, and one draw needn't show every extreme that they name: Passage lengths; some passage has exactly 256 tokens in every draw. Every group number is the owner of exactly 2 passages.
All inputs are finite; a program needn't handle non-finite values.
Results may differ from a plain program's by a relative error of at most 0.0095.
Values may be sent and summed in bfloat16 or wider, within the bound.
No kernel may reach another device: no remote copies, remote signals or barrier semaphores. Data moves between devices by JAX's collectives and lax.ppermute only.
A program may use at most 192 MiB of HBM per device.

v0:
```python
import math

import jax
import jax.numpy as jnp
from jax import lax
from jax.sharding import PartitionSpec as P

H = 64
KVH = 8
HD = 128


def local(queries, cand_kv, prefix_kv, lengths, owner):
    ratio = H // KVH
    inv_root = 1.0 / math.sqrt(HD)
    heads_dev = queries.shape[2] // HD
    group_heads = min(heads_dev, ratio)
    kv_dev = heads_dev // group_heads
    ranked = jnp.argsort(owner, stable=True)
    sent_q = jnp.take(queries, ranked, axis=0)
    sent_kv = jnp.take(cand_kv, ranked, axis=0)
    mine_q, mine_kv = (
        lax.all_to_all(sent_q, "group", split_axis=0, concat_axis=1, tiled=True),
        lax.all_to_all(sent_kv, "group", split_axis=0, concat_axis=1, tiled=True),
    )
    passes = mine_q.shape[0]
    plen_full = mine_q.shape[1]
    row_count = passes * plen_full
    sorted_len = jnp.take(lengths, ranked, axis=0)
    own_lens = lax.dynamic_slice_in_dim(sorted_len, lax.axis_index("group") * passes, passes)
    head_first = lax.axis_index("prefix") * heads_dev
    kv_first = head_first // ratio
    own_keys = lax.dynamic_slice_in_dim(mine_kv, kv_first * HD, kv_dev * HD, 2).reshape(
        passes, plen_full, kv_dev, HD
    )
    own_vals = lax.dynamic_slice_in_dim(mine_kv, KVH * HD + kv_first * HD, kv_dev * HD, 2).reshape(
        passes, plen_full, kv_dev, HD
    )
    my_q = mine_q.reshape(passes, plen_full, kv_dev, group_heads, HD)
    own_scores = (
        jnp.einsum("ptkgd,pskd->pkgts", my_q, own_keys, preferred_element_type=jnp.float32)
        * inv_root
    )
    positions = jnp.arange(plen_full, dtype=jnp.int32)
    causal = positions[None, :] <= positions[:, None]
    allowed = causal[None, :, :] & (positions[None, None, :] < own_lens[:, None, None])
    allowed = allowed[:, None, None, :, :]
    own_top = jnp.max(jnp.where(allowed, own_scores, -jnp.inf), axis=-1)
    shifted = jnp.minimum(own_scores - own_top[..., None], 0.0)
    own_weights = jnp.where(allowed, jnp.exp(shifted), 0.0).astype(jnp.bfloat16)
    own_total = jnp.sum(own_weights.astype(jnp.float32), axis=-1)
    own_out = jnp.einsum(
        "pkgts,pskd->pkgtd", own_weights, own_vals, preferred_element_type=jnp.float32
    )
    whole_q = lax.all_gather(mine_q, "prefix", axis=2, tiled=True).reshape(row_count, H * HD)
    maxima_list = []
    totals_list = []
    outputs_list = []
    for head_index in range(KVH):
        head_q = whole_q[:, head_index * ratio * HD : (head_index + 1) * ratio * HD].reshape(
            row_count, ratio, HD
        )
        head_k = prefix_kv[:, head_index * HD : (head_index + 1) * HD]
        head_v = prefix_kv[:, (KVH + head_index) * HD : (KVH + head_index + 1) * HD]
        head_scores = (
            jnp.einsum("rgd,kd->rgk", head_q, head_k, preferred_element_type=jnp.float32) * inv_root
        )
        head_top = jnp.max(head_scores, axis=-1)
        head_weights = jnp.exp(head_scores - head_top[..., None]).astype(jnp.bfloat16)
        totals_list.append(jnp.sum(head_weights.astype(jnp.float32), axis=-1))
        outputs_list.append(
            jnp.einsum("rgk,kd->rgd", head_weights, head_v, preferred_element_type=jnp.float32)
        )
        maxima_list.append(head_top)
    local_max = jnp.stack(maxima_list, axis=1).reshape(row_count, H)
    local_total = jnp.stack(totals_list, axis=1).reshape(row_count, H)
    local_out = jnp.stack(outputs_list, axis=1).reshape(row_count, H, HD)
    row_top = lax.pmax(local_max, "prefix")
    factor = jnp.exp(local_max - row_top)
    summed_out, summed_total = (
        lax.psum_scatter(local_out * factor[..., None], "prefix", scatter_dimension=1, tiled=True),
        lax.psum_scatter(local_total * factor, "prefix", scatter_dimension=1, tiled=True),
    )
    mine_top = lax.dynamic_slice_in_dim(row_top, head_first, heads_dev, 1)
    pre_top = mine_top.reshape(passes, plen_full, kv_dev, group_heads).transpose(0, 2, 3, 1)
    pre_total = summed_total.reshape(passes, plen_full, kv_dev, group_heads).transpose(0, 2, 3, 1)
    pre_out = summed_out.reshape(passes, plen_full, kv_dev, group_heads, HD).transpose(
        0, 2, 3, 1, 4
    )
    joint = jnp.maximum(pre_top, own_top)
    pre_factor = jnp.exp(pre_top - joint)
    own_factor = jnp.exp(own_top - joint)
    numer = pre_out * pre_factor[..., None] + own_out * own_factor[..., None]
    denom = pre_total * pre_factor + own_total * own_factor
    result = numer / denom[..., None]
    result = result.transpose(0, 3, 1, 2, 4).reshape(passes, plen_full, heads_dev * HD)
    valid = positions[None, :, None] < own_lens[:, None, None]
    return jnp.where(valid, result, 0.0).astype(jnp.bfloat16)


def solution(mesh):
    return jax.shard_map(
        local,
        mesh=mesh,
        in_specs=(P(None, "group", "prefix"), P(None, "group", None), P("prefix", None), P(), P()),
        out_specs=P("group", None, "prefix"),
        check_vma=False,
    )
```

profile of v0, /device:TPU:1, one launch (start us, length us, event | category | flops | bytes accessed | tf_op | source)
XLA Modules:
  0.0 511.4 jit_solution(15697539171553138096)
XLA Ops:
  6.5 2.0 sort.17
  8.6 1.3 gather_fusion
  9.9 1.6 gather_fusion.1
  11.6 0.1 broadcast_select_fusion.1
  11.7 15.0 %all_to_all.36 = bf16[16,32,512]{2,1,0:T(8,128)(2,1)S(1)} all-to-all(bf16[16,32,512]{2,1,0:T(8,128)(2,1)S(1)} %broadcast_select_fusion.1), channel_id=1, replica_groups=mesh['prefix'=16,'group'=8] {'group'}, dimensions={0} | all-to-all | bytes 1048576 | tf_op jit(solution)/shard_map/all_to_all | solution.py:23
  26.6 0.8 copy.56
  27.5 78.6 %all-gather.2.cloned.1.call-done = bf16[2,256,8192]{2,1,0:T(8,128)(2,1)} async-done(((bf16[2,256,512]{2,1,0:T(8,128)(2,1)}), bf16[2,256,8192]{2,1,0:T(8,128)(2,1)}) %all-gather.2.cloned.1.call-update) | async-done | bytes 8388624 | tf_op jit(solution)/shard_map/all_gather | solution.py:55
  106.2 6.0 %fusion.72 = (bf16[512,1024]{1,0:T(8,128)(2,1)}, bf16[512,1024]{1,0:T(8,128)(2,1)}, bf16[512,1024]{1,0:T(8,128)(2,1)}, bf16[512,1024]{1,0:T(8,128)(2,1)}, bf16[5...) fusion(bf16[512,8192]{1,0:T(8,128)(2,1)} %bitcast.225), kind=kLoop, calls=%fused_computation.145 | loop fusion | bytes 16777216 | tf_op jit(solution)/shard_map/slice | solution.py:60
  112.2 1.3 copy.94
  113.5 3.7 multiply_reduce_fusion.7
  117.2 3.7 convert_reduce_fusion.7
  120.9 5.3 %bitcast_dynamic-update-slice_fusion.7 = f32[512,8,8,128]{3,0,2,1:T(8,128)} fusion(f32[512,8,1024]{2,0,1:T(8,128)S(1)} %get-tuple-element.23, f32[512,8]{0,1:T(8,128)S(1)} %get-tuple-element.22, bf16[1024,2048]{1,0:T(8,128)(2,1)} %param.7), kind=kOutput, calls=%fused_computation.42 | convolution fusion | flops 1086324736 | bytes 19152896 | tf_op jit(solution)/shard_map/rgk,kd->rgd/dot_general | solution.py:72
  126.2 1.5 copy.101
  127.7 2.3 copy.100
  130.0 2.3 copy.99
  132.3 2.3 copy.98
  134.6 2.3 copy.97
  136.9 2.3 copy.96
  139.2 2.3 copy.95
  141.5 3.9 multiply_reduce_fusion.6
  145.4 3.7 convert_reduce_fusion.6
  149.1 4.5 bitcast_dynamic-update-slice_fusion.6
  153.6 2.4 multiply_reduce_fusion.5
  156.0 3.7 convert_reduce_fusion.5
  159.7 4.3 bitcast_dynamic-update-slice_fusion.5
  164.1 2.4 multiply_reduce_fusion.4
  166.5 3.7 convert_reduce_fusion.4
  170.2 4.7 bitcast_dynamic-update-slice_fusion.4
  174.9 2.5 multiply_reduce_fusion.3
  177.4 3.7 convert_reduce_fusion.3
  181.0 4.3 bitcast_dynamic-update-slice_fusion.3
  185.4 2.5 multiply_reduce_fusion.2
  187.8 3.7 convert_reduce_fusion.2
  191.5 4.4 bitcast_dynamic-update-slice_fusion.2
  196.0 2.5 multiply_reduce_fusion.1
  198.4 3.7 convert_reduce_fusion.1
  202.1 4.3 bitcast_dynamic-update-slice_fusion.1
  206.4 2.4 multiply_reduce_fusion
  208.9 3.7 convert_reduce_fusion
  212.5 4.3 bitcast_dynamic-update-slice_fusion
  217.0 81.0 %all-reduce.4.cloned.1.call-done = f32[512,64]{0,1:T(8,128)} async-done(((f32[512,64]{0,1:T(8,128)}), f32[512,64]{0,1:T(8,128)}) %all-reduce.4.cloned.1.call-update) | async-done | bytes 131088 | tf_op jit(solution)/shard_map/pmax | solution.py:78
  298.0 1.6 bitcast_multiply_fusion.2
  299.8 12.7 %bitcast_multiply_fusion = f32[512,64,128]{2,0,1:T(8,128)} fusion(f32[512,8,8,128]{3,0,2,1:T(8,128)} %bitcast_dynamic-update-slice_fusion, f32[512,64]{0,1:T(8,128)S(1)} %get-tuple-element.8), kind=kLoop, calls=%fused_computation.3 | loop fusion | flops 4194304 | bytes 33685504 | tf_op jit(solution)/shard_map/mul | solution.py:81
  312.5 2.0 gather_fusion.2
  314.5 3.2 broadcast_select_fusion
  317.6 6.7 %all-to-all-start.1 = ((bf16[16,32,2048]{2,1,0:T(8,128)(2,1)}), bf16[16,32,2048]{2,1,0:T(8,128)(2,1)}, u32[]{:S(2)}, u32[]{:S(2)}) async-start(bf16[16,32,2048]{2,1,0:T(8,128)(2,1)} %broadcast_select_fusion), calls=%async_computation.2 | async-start | bytes 4194304 | tf_op jit(solution)/shard_map/all_to_all | solution.py:24
  324.4 0.6 dynamic-slice
  325.7 0.1 dynamic_slice.12
  325.8 0.1 iota_compare_fusion.1
  325.8 0.1 broadcast_and_fusion
  326.0 0.1 reshape.170
  326.1 24.6 %all-to-all-done.1 = bf16[16,32,2048]{2,1,0:T(8,128)(2,1)} async-done(((bf16[16,32,2048]{2,1,0:T(8,128)(2,1)}), bf16[16,32,2048]{2,1,0:T(8,128)(2,1)}, u32[]{:S(2)}, u32[]{:S(2)}) %all-to-all-start.1) | async-done | bytes 2097184 | tf_op jit(solution)/shard_map/all_to_all | solution.py:24
  350.7 1.7 copy.74
  352.5 0.5 fusion
  353.0 1.4 copy-done.1
  354.4 0.5 convert_reduce_fusion.8
  355.0 0.7 constant_dynamic-slice_fusion
  355.7 27.6 %all-reduce.6.cloned.1.call-done = f32[512,64]{0,1:T(8,128)} async-done(((f32[512,64]{0,1:T(8,128)}), f32[512,64]{0,1:T(8,128)}) %all-reduce.6.cloned.1.call-update) | async-done | bytes 131088
  383.3 0.7 constant_dynamic-slice_fusion.1
  384.0 113.8 %reduce-scatter.2.cloned.1.call-done = f32[512,4,128]{2,0,1:T(8,128)} async-done(((f32[512,64,128]{2,0,1:T(8,128)}), f32[512,4,128]{2,0,1:T(8,128)}) %reduce-scatter.2.cloned.1.call-update) | async-done | bytes 1048592 | tf_op jit(solution)/shard_map/reduce_scatter | solution.py:81
  497.8 1.6 copy.73
  499.3 3.0 fusion.7
  502.4 1.3 copy.80
  503.6 1.0 select_convert_fusion
  (53 shorter events, 0.4 us)
Async XLA Ops:
  6.5 305.9 %copy-start = (bf16[16,32,2048]{2,1,0:T(8,128)(2,1)S(1)}, bf16[16,32,2048]{2,1,0:T(8,128)(2,1)}, u32[]{:S(2)}) copy-start(bf16[16,32,2048]{2,1,0:T(8,128)(2,1)} %param.6) | copy-start | bytes 6291460
  6.5 99.7 %all-gather.2.cloned.1.call-start = ((), (), s32[]{:S(2)}) async-start(), calls=%async_computation.3 | async-start | bytes 8912896 | tf_op jit(solution)/shard_map/all_gather | solution.py:55
  27.5 270.5 %all-reduce.4.cloned.1.call-start = ((), (), s32[]{:S(2)}) async-start(), calls=%async_computation.4 | async-start | bytes 262144 | tf_op jit(solution)/shard_map/pmax | solution.py:78
  141.5 7.5 %copy-start.3 = (bf16[1024,2048]{1,0:T(8,128)(2,1)S(1)}, bf16[1024,2048]{1,0:T(8,128)(2,1)}, u32[]{:S(2)}) copy-start(bf16[1024,2048]{1,0:T(8,128)(2,1)} %param.7) | copy-start | bytes 12582916
  145.4 8.2 %copy-start.8 = (bf16[512,1024]{0,1:T(8,128)(2,1)S(1)}, bf16[512,1024]{0,1:T(8,128)(2,1)}, u32[]{:S(2)}) copy-start(bf16[512,1024]{0,1:T(8,128)(2,1)} %copy.96) | copy-start | bytes 3145732
  156.0 8.0 %copy-start.7 = (bf16[512,1024]{0,1:T(8,128)(2,1)S(1)}, bf16[512,1024]{0,1:T(8,128)(2,1)}, u32[]{:S(2)}) copy-start(bf16[512,1024]{0,1:T(8,128)(2,1)} %copy.97) | copy-start | bytes 3145732
  166.5 8.4 %copy-start.6 = (bf16[512,1024]{0,1:T(8,128)(2,1)S(1)}, bf16[512,1024]{0,1:T(8,128)(2,1)}, u32[]{:S(2)}) copy-start(bf16[512,1024]{0,1:T(8,128)(2,1)} %copy.98) | copy-start | bytes 3145732
  177.4 8.0 %copy-start.5 = (bf16[512,1024]{0,1:T(8,128)(2,1)S(1)}, bf16[512,1024]{0,1:T(8,128)(2,1)}, u32[]{:S(2)}) copy-start(bf16[512,1024]{0,1:T(8,128)(2,1)} %copy.99) | copy-start | bytes 3145732
  187.8 8.1 %copy-start.4 = (bf16[512,1024]{0,1:T(8,128)(2,1)S(1)}, bf16[512,1024]{0,1:T(8,128)(2,1)}, u32[]{:S(2)}) copy-start(bf16[512,1024]{0,1:T(8,128)(2,1)} %copy.100) | copy-start | bytes 3145732
  208.9 8.0 %copy-start.10 = (f32[512,8,8]{0,2,1:T(8,128)}, f32[512,8,8]{0,2,1:T(8,128)S(1)}, u32[]{:S(2)}) copy-start(f32[512,8,8]{0,2,1:T(8,128)S(1)} %constant_dynamic-update-slice_fusion) | copy-start | bytes 393220
  216.9 166.4 %all-reduce.6.cloned.1.call-start = ((), (), s32[]{:S(2)}) async-start(), calls=%async_computation.6 | async-start | bytes 262144
  299.7 198.1 %reduce-scatter.2.cloned.1.call-start = ((), (), s32[]{:S(2)}) async-start(), calls=%async_computation.5 | async-start | bytes 17825792 | tf_op jit(solution)/shard_map/reduce_scatter | solution.py:81
  312.4 12.0 %copy-start.11 = (u32[128]{0:T(128)S(1)}, u32[128]{0:T(128)}, u32[]{:S(2)}) copy-start(u32[128]{0:T(128)} %constant.91) | copy-start | bytes 1540
  312.4 13.6 %copy-start.2 = (bf16[2,8,32,512]{3,2,1,0:T(8,128)(2,1)S(1)}, bf16[2,8,32,512]{3,2,1,0:T(8,128)(2,1)}, u32[]{:S(2)}) copy-start(bf16[2,8,32,512]{3,2,1,0:T(8,128)(2,1)} %copy.56) | copy-start | bytes 1572868
  317.6 33.1 %all-to-all-start.1 = ((bf16[16,32,2048]{2,1,0:T(8,128)(2,1)}), bf16[16,32,2048]{2,1,0:T(8,128)(2,1)}, u32[]{:S(2)}, u32[]{:S(2)}) async-start(bf16[16,32,2048]{2,1,0:T(8,128)(2,1)} %broadcast_select_fusion), calls=%async_computation.2 | async-start | bytes 4194304 | tf_op jit(solution)/shard_map/all_to_all | solution.py:24
  352.5 2.5 copy-start.9
  353.0 1.4 copy-start.1
Sparse Core Ops, SparseCore 0:
  27.6 78.5 all-gather.1
  217.0 81.0 all-reduce.3
  301.6 81.6 all-reduce.5
  386.5 111.1 reduce-scatter.1
where the time goes:
time: 520 us; the launch traced here: 511 us
  waiting for transfers between devices  326 us (63%)
  matrix products  62 us (12%)
  other arithmetic  50.7 us (10%)
  local copies, waits for them, and re-layouts  36.7 us (7%)
  blocking collectives  15 us (3%)
  between operations  14.4 us (3%)
  starting transfers between devices  6.88 us (1%)
    reduce_scatter x1, waiting for transfers between devices, local(): lax.psum_scatter(local_out * factor[..., None], 'prefix', scatter_dimensi...  114 us
    pmax x1, waiting for transfers between devices, local(): row_top = lax.pmax(local_max, 'prefix')  81 us
    all_gather x1, waiting for transfers between devices, local(): lax.all_gather(mine_q, 'prefix', axis=2, tiled=True)  78.6 us
    dot_general x8, matrix products, local(): jnp.einsum('rgk,kd->rgd', head_weights, head_v, preferred_element_type=jn...  36.2 us
    reduce_sum x8, other arithmetic, local(): totals_list.append(jnp.sum(head_weights.astype(jnp.float32), axis=-1))  29.3 us
    unnamed x5, waiting for transfers between devices  27.6 us
    all_to_all x1, waiting for transfers between devices, local(): lax.all_to_all(sent_kv, 'group', split_axis=0, concat_axis=1, tiled=True)  24.6 us
    dot_general x8, matrix products, local(): jnp.einsum('rgd,kd->rgk', head_q, head_k, preferred_element_type=jnp.floa...  22.3 us
  transfers between devices with their start and end apart: 5, of which 5 were waited for; matrix products, arithmetic and copies ran while one was open for 5% of the time, Pallas kernels for 0%

commit v1 on v0

v1 whole, which is shorter than its diff:
```python
import functools
import math

import jax
import jax.numpy as jnp
from jax import lax
from jax.experimental import pallas as pl
from jax.experimental.pallas import tpu as pltpu
from jax.sharding import PartitionSpec as P

H = 64
KVH = 8
HD = 128
NT = (((1,), (1,)), ((), ()))
NN = (((1,), (0,)), ((), ()))
SCALE = math.log2(math.e) / math.sqrt(HD)
LOW = -1e30
VMEM = pl.BlockSpec(memory_space=pltpu.VMEM)
SMEM = pl.BlockSpec(memory_space=pltpu.SMEM)
ANY = pl.BlockSpec(memory_space=pl.ANY)
LIMIT = 56 * 2**20
TB = 32
RB = 4
KB = 512


def run_all(copies):
    for copy in copies:
        copy.start()
    for copy in copies:
        copy.wait()


def prep_kernel(info, q, cand, kv, csend, kvsend, sem):
    head = pl.multiple_of(info[0] * HD, HD)
    rows = pl.ds(pl.multiple_of(info[3] * HD, HD), HD)
    copies = [
        pltpu.make_async_copy(q, csend.at[:, :, 0:512], sem.at[0]),
        pltpu.make_async_copy(cand.at[:, :, pl.ds(head, HD)], csend.at[:, :, 512:640], sem.at[1]),
        pltpu.make_async_copy(
            cand.at[:, :, pl.ds(pl.multiple_of(head + KVH * HD, HD), HD)],
            csend.at[:, :, 640:768],
            sem.at[2],
        ),
    ]
    for dest in range(16):
        for half in range(2):
            column = (half * KVH + dest // 2) * HD
            copies.append(
                pltpu.make_async_copy(
                    kv.at[rows, column : column + HD],
                    kvsend.at[dest, :, half * HD : (half + 1) * HD],
                    sem.at[3 + dest * 2 + half],
                )
            )
    run_all(copies)


def prep(info, q, cand, kv):
    return pl.pallas_call(
        prep_kernel,
        out_shape=(
            jax.ShapeDtypeStruct((16, 32, 768), jnp.bfloat16),
            jax.ShapeDtypeStruct((16, 128, 256), jnp.bfloat16),
        ),
        in_specs=[SMEM, ANY, ANY, ANY],
        out_specs=(ANY, ANY),
        scratch_shapes=[pltpu.SemaphoreType.DMA((35,))],
        name="prep",
    )(info, q, cand, kv)


def pack_kernel(owner, info, mine, other, b0, b1, b2, b3, count, sem):
    x, core = info[1], info[2]
    bufs = (b0, b1, b2, b3)
    for o in range(8):
        count[o] = 0

    def each(act):
        for i in range(16):
            o = owner[i]
            slot = count[o]
            count[o] = slot + 1
            ox = o // 2

            @pl.when(o % 2 == core)
            def _(i=i, slot=slot, ox=ox):
                def block(src, source_core):
                    row = pl.multiple_of(ox * 128 + slot * 64 + source_core * 32, 32)
                    for b in range(4):
                        act(src.at[i, :, 0:512], bufs[b].at[pl.ds(row, 32), :], b)
                    for b in range(4):

                        @pl.when(ox == lax.rem(x + b, 4))
                        def _(b=b):
                            act(
                                src.at[i, :, 512:768],
                                bufs[b].at[
                                    pl.ds(pl.multiple_of(512 + source_core * 32, 32), 32),
                                    pl.ds(pl.multiple_of(slot * 256, 256), 256),
                                ],
                                4 + b,
                            )

                block(mine, core)
                block(other, 1 - core)

    each(lambda s, d, k: pltpu.make_async_copy(s, d, sem.at[k]).start())
    for b in range(4):
        pltpu.make_async_copy(bufs[b].at[0:512, :], bufs[b].at[0:512, :], sem.at[b]).wait()
        pltpu.make_async_copy(bufs[b].at[512:576, :], bufs[b].at[512:576, :], sem.at[4 + b]).wait()


def pack(owner, info, mine, other):
    return pl.pallas_call(
        pack_kernel,
        out_shape=(jax.ShapeDtypeStruct((576, 512), jnp.bfloat16),) * 4,
        in_specs=[SMEM, SMEM, ANY, ANY],
        out_specs=(ANY,) * 4,
        scratch_shapes=[pltpu.SMEM((8,), jnp.int32), pltpu.SemaphoreType.DMA((8,))],
        name="pack",
    )(owner, info, mine, other)


def slot_lengths(owner, lengths, group):
    first, second, seen = 0, 0, 0
    for i in range(16):
        hit = owner[i] == group
        first = jnp.where(hit & (seen == 0), lengths[i], first)
        second = jnp.where(hit & (seen == 1), lengths[i], second)
        seen = seen + hit.astype(jnp.int32)
    return first, second


def pieces(v):
    hi = v.astype(jnp.bfloat16).astype(jnp.float32)
    mid = (v - hi).astype(jnp.bfloat16).astype(jnp.float32)
    return hi, mid, v - hi - mid


def flash_kernel(shift, own, owner, lengths, info, b0, b1, b2, b3, kv0, kv1, *rest):
    if own:
        out, stats, qraw, okv, qs, v1, sem = rest
    else:
        out, qraw, qs, v1, sem = rest
    x, core = info[1], info[2]
    dest = lax.rem(x + shift, 4)
    len0, len1 = slot_lengths(owner, lengths, dest * 2 + core)
    copies = []
    for b, buf in enumerate((b0, b1, b2, b3)):
        source = lax.rem(x + 4 - b, 4)
        rows = pl.ds(pl.multiple_of(dest * 128, 128), 128)
        copies.append(pltpu.make_async_copy(buf.at[rows, :], qraw.at[source], sem.at[b]))
        if own:
            copies.append(pltpu.make_async_copy(buf.at[512:576, :], okv.at[source], sem.at[4 + b]))
    for c in copies:
        c.start()
    for half, kv in enumerate((kv0, kv1)):
        v1[half * 2048 : (half + 1) * 2048, 0:HD] = kv[:, HD : 2 * HD]
    v1[:, HD : 2 * HD] = jnp.ones((4096, HD), jnp.bfloat16)
    for c in copies:
        c.wait()
    n0 = lax.div(len0 + (TB - 1), TB)
    total = n0 + lax.div(len1 + (TB - 1), TB)

    def place(n):
        slot = (n >= n0).astype(jnp.int32)
        return slot, n - slot * n0

    @pl.loop(0, total)
    def _(n):
        slot, tb = place(n)
        rows = pl.ds(pl.multiple_of(slot * 64 + lax.rem(tb, 2) * TB, TB), TB)
        block = lax.div(n, RB)
        base = lax.rem(n, RB) * TB
        for h in range(4):
            qs[block, pl.ds(pl.multiple_of(h * RB * TB + base, TB), TB), :] = qraw[
                lax.div(tb, 2), rows, h * HD : (h + 1) * HD
            ]

    rows_of = 4 * RB * TB

    @pl.loop(0, lax.div(total + (RB - 1), RB))
    def _(rb):
        q = qs[rb]
        top = jnp.full((rows_of, 1), LOW, jnp.float32)
        acc = jnp.zeros((rows_of, 2 * HD), jnp.float32)

        def step(s, v, top, acc):
            new = jnp.maximum(top, jnp.max(s, axis=1, keepdims=True) * SCALE)
            p = jnp.exp2(s * SCALE - new).astype(jnp.bfloat16)
            acc = acc * jnp.exp2(top - new) + lax.dot_general(
                p, v, NN, preferred_element_type=jnp.float32
            )
            return new, acc

        if own:
            kv_rows = [okv[a, :, 0:512] for a in range(4)]
            keys = jnp.concatenate(
                [r[:, s * 256 : s * 256 + HD] for s in range(2) for r in kv_rows], axis=0
            )
            vals = jnp.concatenate(
                [r[:, s * 256 + HD : s * 256 + 2 * HD] for s in range(2) for r in kv_rows], axis=0
            )
            vals = jnp.concatenate([vals, jnp.ones((512, HD), jnp.bfloat16)], axis=1)
            s = lax.dot_general(q, keys, NT, preferred_element_type=jnp.float32)
            firsts, lasts = [], []
            for i in range(RB):
                slot, tb = place(rb * RB + i)
                first = jnp.full((TB, 1), slot * 256, jnp.int32)
                firsts.append(first)
                lasts.append(first + tb * TB + lax.broadcasted_iota(jnp.int32, (TB, 1), 0))
            first = jnp.concatenate(firsts * 4, axis=0)
            last = jnp.concatenate(lasts * 4, axis=0)
            place_of = lax.broadcasted_iota(jnp.int32, (rows_of, 512), 1)
            allowed = (place_of >= first) & (place_of <= last)
            s = jnp.where(allowed, s, LOW)
            new = jnp.max(s, axis=1, keepdims=True) * SCALE
            p = jnp.where(allowed, jnp.exp2(jnp.minimum(s * SCALE - new, 0.0)), 0.0)
            acc = lax.dot_general(
                p.astype(jnp.bfloat16), vals, NN, preferred_element_type=jnp.float32
            )
            top = new
        for half, kv in enumerate((kv0, kv1)):
            for j in range(2048 // KB):
                s = lax.dot_general(
                    q, kv[j * KB : (j + 1) * KB, 0:HD], NT, preferred_element_type=jnp.float32
                )
                start = half * 2048 + j * KB
                top, acc = step(s, v1[start : start + KB, :], top, acc)
        lane = lax.broadcasted_iota(jnp.int32, (TB, HD), 1)
        for i in range(RB):
            n = rb * RB + i

            @pl.when(n < total)
            def _(i=i, n=n):
                slot, tb = place(n)
                rows = pl.ds(pl.multiple_of(slot * 256 + tb * TB, TB), TB)
                st = jnp.zeros((TB, HD), jnp.float32)
                for h in range(4):
                    r = h * RB * TB + i * TB
                    a = acc[r : r + TB, :]
                    out[rows, h * HD : (h + 1) * HD] = a[:, 0:HD].astype(out.dtype)
                    t = jnp.broadcast_to(top[r : r + TB, :], (TB, HD))
                    for k, piece in enumerate(pieces(t) + pieces(a[:, HD : 2 * HD])):
                        st = jnp.where(lane == h * 8 + k, piece, st)
                if own:
                    stats[rows, :] = st.astype(jnp.bfloat16)
                else:
                    out[rows, 512:640] = st.astype(jnp.bfloat16)


def flash(shift, owner, lengths, info, bufs, kv0, kv1):
    own = shift == 0
    scratch = [pltpu.VMEM((4, 128, 512), jnp.bfloat16)]
    if own:
        scratch.append(pltpu.VMEM((4, 64, 512), jnp.bfloat16))
        out_shape = (
            jax.ShapeDtypeStruct((512, 512), jnp.float32),
            jax.ShapeDtypeStruct((512, 128), jnp.bfloat16),
        )
        out_specs = (VMEM, VMEM)
    else:
        out_shape = jax.ShapeDtypeStruct((512, 640), jnp.bfloat16)
        out_specs = VMEM
    scratch += [
        pltpu.VMEM((16 // RB, 4 * RB * TB, HD), jnp.bfloat16),
        pltpu.VMEM((4096, 2 * HD), jnp.bfloat16),
        pltpu.SemaphoreType.DMA((8,)),
    ]
    return pl.pallas_call(
        functools.partial(flash_kernel, shift, own),
        out_shape=out_shape,
        in_specs=[SMEM, SMEM, SMEM, ANY, ANY, ANY, ANY, VMEM, VMEM],
        out_specs=out_specs,
        scratch_shapes=scratch,
        compiler_params=pltpu.CompilerParams(vmem_limit_bytes=LIMIT),
        cost_estimate=pl.CostEstimate(
            flops=2 * 2 * 2048 * 4096 * 256, bytes_accessed=4 * 2**20, transcendentals=2048 * 4096
        ),
        name="flash_own" if own else "flash",
    )(owner, lengths, info, *bufs, kv0, kv1)


def combine_kernel(owner, lengths, info, acc, stats, g1, g2, g3, out):
    step = pl.program_id(0)
    len0, len1 = slot_lengths(owner, lengths, info[3])
    lane = lax.broadcasted_iota(jnp.int32, (HD, 1024), 0)
    col = lax.broadcasted_iota(jnp.int32, (HD, 1024), 1)
    kind = lane % 8 - 3 * (col // 512)
    pick = (lane // 8 == (col % 512) // HD) & (kind >= 0) & (kind < 3)
    pick = pick.astype(jnp.float32).astype(jnp.bfloat16)
    parts = [(acc[...], stats[...])] + [
        (g[:, 0:512].astype(jnp.float32), g[:, 512:640]) for g in (g1, g2, g3)
    ]
    wide = [lax.dot_general(st, pick, NN, preferred_element_type=jnp.float32) for _, st in parts]
    top = functools.reduce(jnp.maximum, [w[:, 0:512] for w in wide])
    numer, denom = 0.0, 0.0
    for (o, _), w in zip(parts, wide):
        f = jnp.exp2(w[:, 0:512] - top)
        numer = numer + o * f
        denom = denom + w[:, 512:1024] * f
    token = lax.rem(step, 2) * 128 + lax.broadcasted_iota(jnp.int32, (128, 1), 0)
    valid = token < jnp.where(step < 2, len0, len1)
    out[...] = jnp.where(valid, numer / denom, 0.0).astype(jnp.bfloat16)


def combine(owner, lengths, info, acc, stats, got):
    rows = lambda width: pl.BlockSpec((128, width), lambda i: (i, 0))
    return pl.pallas_call(
        combine_kernel,
        grid=(4,),
        out_shape=jax.ShapeDtypeStruct((512, 512), jnp.bfloat16),
        in_specs=[SMEM, SMEM, SMEM, rows(512), rows(128), rows(640), rows(640), rows(640)],
        out_specs=rows(512),
        compiler_params=pltpu.CompilerParams(vmem_limit_bytes=LIMIT),
        name="combine",
    )(owner, lengths, info, acc, stats, *got)


CORE = [(i, i ^ 1) for i in range(8)]


def along_x(shift):
    return [(i, (i + 2 * shift) % 8) for i in range(8)]


def local(queries, cand_kv, prefix_kv, lengths, owner):
    g = lax.axis_index("group")
    info = jnp.stack([lax.axis_index("prefix") // 2, g // 2, g % 2, g]).astype(jnp.int32)
    csend, kvsend = prep(info, queries, cand_kv, prefix_kv)
    crecv = lax.ppermute(csend, "group", CORE)
    b0, s1, s2, s3 = pack(owner, info, csend, crecv)
    b2 = lax.ppermute(s2, "group", along_x(2))
    b1 = lax.ppermute(s1, "group", along_x(1))
    b3 = lax.ppermute(s3, "group", along_x(3))
    bufs = (b0, b1, b2, b3)
    kv0 = lax.all_to_all(kvsend, "prefix", split_axis=0, concat_axis=0, tiled=True)
    kv0 = kv0.reshape(2048, 256)
    kv1 = lax.ppermute(kv0, "group", CORE)
    got = []
    for shift in (2, 1, 3):
        o = flash(shift, owner, lengths, info, bufs, kv0, kv1)
        got.append(lax.ppermute(o, "group", along_x(shift)))
    acc, stats = flash(0, owner, lengths, info, bufs, kv0, kv1)
    return combine(owner, lengths, info, acc, stats, got).reshape(2, 256, 512)


def solution(mesh):
    return jax.shard_map(
        local,
        mesh=mesh,
        in_specs=(P(None, "group", "prefix"), P(None, "group", None), P("prefix", None), P(), P()),
        out_specs=P("group", None, "prefix"),
        check_vma=False,
    )
```

time: 520 us -> 264 us (0.51); the launches traced: 511 us -> 266 us
  waiting for transfers between devices: 326 us -> 40.1 us
  Pallas kernels: 0 us -> 198 us
  matrix products: 62 us -> 0 us
  other arithmetic: 50.7 us -> 0.67 us
  local copies, waits for them, and re-layouts: 36.7 us -> 3.42 us
  starting transfers between devices: 6.88 us -> 23.3 us
  blocking collectives: 15 us -> 0 us
  between operations: 14.4 us -> 0.15 us
    pallas_call x0 -> x7, Pallas kernels: none -> 198 us  [the longest x1 73.4 us: pack(): pl.pallas_call(pack_kernel, out_shape=(jax.ShapeDtypeStruct((576, 512), j...]
    reduce_scatter x1 -> x0, waiting for transfers between devices: 114 us -> none  [local(): lax.psum_scatter(local_out * factor[..., None], 'prefix', scatter_dimensi...]
    pmax x1 -> x0, waiting for transfers between devices: 81 us -> none  [local(): row_top = lax.pmax(local_max, 'prefix')]
    all_gather x1 -> x0, waiting for transfers between devices: 78.6 us -> none  [local(): lax.all_gather(mine_q, 'prefix', axis=2, tiled=True)]
    dot_general x18 -> x0, matrix products: 62 us -> none  [the longest x8 36.2 us: local(): jnp.einsum('rgk,kd->rgd', head_weights, head_v, preferred_element_type=jn...]
    reduce_sum x9 -> x0, other arithmetic: 29.8 us -> none  [the longest x8 29.3 us: local(): totals_list.append(jnp.sum(head_weights.astype(jnp.float32), axis=-1))]
    unnamed x5 -> x0, waiting for transfers between devices: 27.6 us -> none
    ppermute x0 -> x8, waiting for transfers between devices: none -> 25.2 us  [the longest x1 13.6 us: local(): b2 = lax.ppermute(s2, 'group', along_x(2))]
  transfers between devices with their start and end apart: 5 -> 9, of which waited for: 5 -> 3; matrix products, arithmetic and copies ran while one was open for 5% -> 0% of each run, Pallas kernels for 0% -> 45%
where the time goes in v1:
time: 264 us; the launch traced here: 266 us
  Pallas kernels  198 us (75%)
  waiting for transfers between devices  40.1 us (15%)
  starting transfers between devices  23.3 us (9%)
  local copies, waits for them, and re-layouts  3.42 us (1%)
    pallas_call x1, Pallas kernels, pack(): pl.pallas_call(pack_kernel, out_shape=(jax.ShapeDtypeStruct((576, 512), j...  73.4 us
    pallas_call x4, Pallas kernels, flash(): pl.pallas_call(functools.partial(flash_kernel, shift, own), out_shape=out...  61.8 us
    pallas_call x1, Pallas kernels, prep(): pl.pallas_call(prep_kernel, out_shape=(jax.ShapeDtypeStruct((16, 32, 768)...  57.7 us
    all_to_all x1, waiting for transfers between devices, local(): lax.all_to_all(kvsend, 'prefix', split_axis=0, concat_axis=0, tiled=True)  14.9 us
    ppermute x1, waiting for transfers between devices, local(): b2 = lax.ppermute(s2, 'group', along_x(2))  13.6 us
    ppermute x1, waiting for transfers between devices, local(): b1 = lax.ppermute(s1, 'group', along_x(1))  11.6 us
    all_to_all x1, starting transfers between devices, local(): lax.all_to_all(kvsend, 'prefix', split_axis=0, concat_axis=0, tiled=True)  8.61 us
    ppermute x3, starting transfers between devices, local(): got.append(lax.ppermute(o, 'group', along_x(shift)))  6.19 us
  transfers between devices with their start and end apart: 9, of which 3 were waited for; matrix products, arithmetic and copies ran while one was open for 0% of the time, Pallas kernels for 45%

profile of v1, /device:TPU:1, one launch (start us, length us, event | category | flops | bytes accessed | tf_op | source)
XLA Modules:
  0.0 265.7 jit_solution(16782059537025503371)
XLA Ops:
  0.0 0.7 pad_add_fusion.info
  0.7 57.7 %prep.1 = (bf16[16,32,768]{2,1,0:T(8,128)(2,1)}, bf16[16,128,256]{2,1,0:T(8,128)(2,1)}) custom-call(s32[4]{0:T(128)} %pad_add_fusion.info, bf16[16,32,512]{2,1,0:T(8,128)(2,1)} %q.1, bf16[16,32,2048]{2,1,0:T(8,128)(2,1)} %cand.1, bf16[1024,2048]{1,0:T(8,128)(2,1)} %kv.1), custom_call_target="tpu_custom_call" | custom-call | tf_op jit(solution)/shard_map/prep/pallas_call | solution.py:60
  58.3 8.6 %all-to-all-start = ((bf16[16,128,256]{2,1,0:T(8,128)(2,1)}), bf16[16,128,256]{2,1,0:T(8,128)(2,1)S(1)}, u32[]{:S(2)}, u32[]{:S(2)}) async-start(bf16[16,128,256]{2,1,0:T(8,128)(2,1)} %get-tuple-element.18), calls=%async_computation | async-start | bytes 2097152 | tf_op jit(solution)/shard_map/all_to_all | solution.py:338
  67.0 1.0 collective-permute-start
  68.0 14.9 %all-to-all-done = bf16[16,128,256]{2,1,0:T(8,128)(2,1)S(1)} async-done(((bf16[16,128,256]{2,1,0:T(8,128)(2,1)}), bf16[16,128,256]{2,1,0:T(8,128)(2,1)S(1)}, u32[]{:S(2)}, u32[]{:S(2)}) %all-to-all-start) | async-done | bytes 1048608 | tf_op jit(solution)/shard_map/all_to_all | solution.py:338
  82.9 0.0 copy-start
  82.9 2.6 collective-permute-start.4
  85.6 0.0 collective-permute-done.other
  85.6 0.0 copy-start.1
  85.6 0.9 copy-done.1
  86.5 73.4 %pack.1 = (bf16[576,512]{1,0:T(8,128)(2,1)}, bf16[576,512]{1,0:T(8,128)(2,1)}, bf16[576,512]{1,0:T(8,128)(2,1)}, bf16[576,512]{1,0:T(8,128)(2,1)}) custom-call(s32[16]{0:T(128)} %owner.11, s32[4]{0:T(128)} %pad_add_fusion.info, bf16[16,32,768]{2,1,0:T(8,128)(2,1)} %get-tuple-element.13.mine, bf16[16,32,768]{2,1,0:T(8,128)(2,1)} %copy-done.1), custom_call_target="tpu_custom_call" | custom-call | tf_op jit(solution)/shard_map/pack/pallas_call | solution.py:115
  159.8 1.3 collective-permute-start.1
  161.1 2.4 collective-permute-start.2
  163.6 1.2 collective-permute-start.3
  164.7 11.6 %collective-permute-done.1.b1 = bf16[576,512]{1,0:T(8,128)(2,1)S(1)} collective-permute-done((bf16[576,512]{1,0:T(8,128)(2,1)}, bf16[576,512]{1,0:T(8,128)(2,1)S(1)}, u32[]{:S(2)}, u32[]{:S(2)}) %collective-permute-start.1) | collective-permute-done | bytes 589856 | tf_op jit(solution)/shard_map/ppermute | solution.py:335
  176.3 0.0 copy-start.6
  176.3 13.6 %collective-permute-done.2.b2 = bf16[576,512]{1,0:T(8,128)(2,1)S(1)} collective-permute-done((bf16[576,512]{1,0:T(8,128)(2,1)}, bf16[576,512]{1,0:T(8,128)(2,1)S(1)}, u32[]{:S(2)}, u32[]{:S(2)}) %collective-permute-start.2) | collective-permute-done | bytes 589856 | tf_op jit(solution)/shard_map/ppermute | solution.py:334
  189.9 0.0 copy-start.7
  189.9 0.0 collective-permute-done.3.b3
  189.9 0.0 copy-start.8
  189.9 0.0 collective-permute-done.4.kv1
  189.9 0.0 copy-start.5
  189.9 0.0 copy-done
  189.9 0.0 copy-done.6
  189.9 0.8 copy-done.7
  190.7 0.2 copy-done.8
  190.9 0.3 copy-done.5
  191.2 16.8 %flash.3 = bf16[512,640]{1,0:T(8,128)(2,1)} custom-call(s32[16]{0:T(128)} %owner.11, s32[16]{0:T(128)} %lengths.9, s32[4]{0:T(128)} %pad_add_fusion.info, bf16[576,512]{1,0:T(8,128)(2,1)} %get-tuple-element.14.b0, bf16[576,512]{1,0:T(8,128)(2,1)} %copy-done.6, bf16[576,512]{1,0:T(8,128)(2,1)} %copy-done.7, bf16[576,512]{1,0:T(8,128)(2,1)} %copy-done.8, ...), custom_call_target="tpu_custom_call" | custom-call | flops 8589934592 | bytes 4194304 | tf_op jit(solution)/shard_map/flash/pallas_call | solution.py:271
  208.0 0.1 collective-permute-start.5
  208.1 16.7 %flash.4 = bf16[512,640]{1,0:T(8,128)(2,1)} custom-call(s32[16]{0:T(128)} %owner.11, s32[16]{0:T(128)} %lengths.9, s32[4]{0:T(128)} %pad_add_fusion.info, bf16[576,512]{1,0:T(8,128)(2,1)} %get-tuple-element.14.b0, bf16[576,512]{1,0:T(8,128)(2,1)} %copy-done.6, bf16[576,512]{1,0:T(8,128)(2,1)} %copy-done.7, bf16[576,512]{1,0:T(8,128)(2,1)} %copy-done.8, ...), custom_call_target="tpu_custom_call" | custom-call | flops 8589934592 | bytes 4194304 | tf_op jit(solution)/shard_map/flash/pallas_call | solution.py:271
  224.9 2.7 %collective-permute-start.6 = (bf16[512,640]{1,0:T(8,128)(2,1)}, bf16[512,640]{1,0:T(8,128)(2,1)S(1)}, u32[]{:S(2)}, u32[]{:S(2)}) collective-permute-start(bf16[512,640]{1,0:T(8,128)(2,1)} %flash.4), channel_id=1, source_target_pairs={{0,2},{1,3},{2,4},{3,5},{4,6},{5,7},{6,0},{7,1},{8,10},{9,11},{10,... | collective-permute-start | bytes 1966088 | tf_op jit(solution)/shard_map/ppermute | solution.py:344
  227.6 13.7 %flash.5 = bf16[512,640]{1,0:T(8,128)(2,1)} custom-call(s32[16]{0:T(128)} %owner.11, s32[16]{0:T(128)} %lengths.9, s32[4]{0:T(128)} %pad_add_fusion.info, bf16[576,512]{1,0:T(8,128)(2,1)} %get-tuple-element.14.b0, bf16[576,512]{1,0:T(8,128)(2,1)} %copy-done.6, bf16[576,512]{1,0:T(8,128)(2,1)} %copy-done.7, bf16[576,512]{1,0:T(8,128)(2,1)} %copy-done.8, ...), custom_call_target="tpu_custom_call" | custom-call | flops 8589934592 | bytes 4194304 | tf_op jit(solution)/shard_map/flash/pallas_call | solution.py:271
  241.3 3.4 %collective-permute-start.7 = (bf16[512,640]{1,0:T(8,128)(2,1)}, bf16[512,640]{1,0:T(8,128)(2,1)S(1)}, u32[]{:S(2)}, u32[]{:S(2)}) collective-permute-start(bf16[512,640]{1,0:T(8,128)(2,1)} %flash.5), channel_id=1, source_target_pairs={{0,6},{1,7},{2,0},{3,1},{4,2},{5,3},{6,4},{7,5},{8,14},{9,15},{10,... | collective-permute-start | bytes 1966088 | tf_op jit(solution)/shard_map/ppermute | solution.py:344
  244.7 14.6 %flash_own.1 = (f32[512,512]{1,0:T(8,128)}, bf16[512,128]{1,0:T(8,128)(2,1)}) custom-call(s32[16]{0:T(128)} %owner.11, s32[16]{0:T(128)} %lengths.9, s32[4]{0:T(128)} %pad_add_fusion.info, bf16[576,512]{1,0:T(8,128)(2,1)} %get-tuple-element.14.b0, bf16[576,512]{1,0:T(8,128)(2,1)} %copy-done.6, bf16[576,512]{1,0:T(8,128)(2,1)} %copy-done.7, ...), custom_call_target="tpu_custom_call" | custom-call | flops 8589934592 | bytes 4194304 | tf_op jit(solution)/shard_map/flash_own/pallas_call | solution.py:271
  259.3 0.0 collective-permute-done.5.g1
  259.3 0.0 copy-start.2
  259.3 0.0 collective-permute-done.6.g2
  259.3 0.0 copy-start.3
  259.3 0.0 collective-permute-done.7.g3
  259.3 0.0 copy-start.4
  259.4 0.8 copy-done.2
  260.2 0.2 copy-done.3
  260.4 0.2 copy-done.4
  260.6 5.1 %combine.1 = bf16[512,512]{1,0:T(8,128)(2,1)} custom-call(s32[16]{0:T(128)} %owner.11, s32[16]{0:T(128)} %lengths.9, s32[4]{0:T(128)} %pad_add_fusion.info, f32[512,512]{1,0:T(8,128)} %get-tuple-element.19.acc, bf16[512,128]{1,0:T(8,128)(2,1)} %get-tuple-element.20.stats, bf16[512,640]{1,0:T(8,128)(2,1)} %copy-done.2, bf16[512,640]{1,0:T(8,128)(2,1)} %copy-done.3, ...), custom_call_target="tpu_custom_call" | custom-call | tf_op jit(solution)/shard_map/combine/pallas_call | solution.py:310
Async XLA Ops:
  58.3 24.6 %all-to-all-start = ((bf16[16,128,256]{2,1,0:T(8,128)(2,1)}), bf16[16,128,256]{2,1,0:T(8,128)(2,1)S(1)}, u32[]{:S(2)}, u32[]{:S(2)}) async-start(bf16[16,128,256]{2,1,0:T(8,128)(2,1)} %get-tuple-element.18), calls=%async_computation | async-start | bytes 2097152 | tf_op jit(solution)/shard_map/all_to_all | solution.py:338
  67.0 18.6 %collective-permute-start = (bf16[16,32,768]{2,1,0:T(8,128)(2,1)}, bf16[16,32,768]{2,1,0:T(8,128)(2,1)S(1)}, u32[]{:S(2)}, u32[]{:S(2)}) collective-permute-start(bf16[16,32,768]{2,1,0:T(8,128)(2,1)} %get-tuple-element.13.mine), channel_id=1, source_target_pairs={{0,1},{1,0},{2,3},{3,2},{4,5},{5,4},{6,7},{7,6},{8,9},{9,8},{10,11... | collective-permute-start | bytes 2359304 | tf_op jit(solution)/shard_map/ppermute | solution.py:332
  82.9 107.0 %copy-start = (bf16[16,128,256]{2,1,0:T(8,128)(2,1)}, bf16[16,128,256]{2,1,0:T(8,128)(2,1)S(1)}, u32[]{:S(2)}) copy-start(bf16[16,128,256]{2,1,0:T(8,128)(2,1)S(1)} %all-to-all-done) | copy-start | bytes 3145732
  82.9 107.0 %collective-permute-start.4 = (bf16[2048,256]{1,0:T(8,128)(2,1)S(1)}, bf16[2048,256]{1,0:T(8,128)(2,1)S(1)}, u32[]{:S(2)}, u32[]{:S(2)}) collective-permute-start(bf16[2048,256]{1,0:T(8,128)(2,1)S(1)} %bitcast.6), channel_id=1, source_target_pairs={{0,1},{1,0},{2,3},{3,2},{4,5},{5,4},{6,7},{7,6},{8,9},{9,8},{10,11... | collective-permute-start | bytes 3145736 | tf_op jit(solution)/shard_map/ppermute | solution.py:340
  85.6 0.9 copy-start.1
  159.8 16.4 %collective-permute-start.1 = (bf16[576,512]{1,0:T(8,128)(2,1)}, bf16[576,512]{1,0:T(8,128)(2,1)S(1)}, u32[]{:S(2)}, u32[]{:S(2)}) collective-permute-start(bf16[576,512]{1,0:T(8,128)(2,1)} %get-tuple-element.15), channel_id=1, source_target_pairs={{0,2},{1,3},{2,4},{3,5},{4,6},{5,7},{6,0},{7,1},{8,10},{9,11},{10,... | collective-permute-start | bytes 1769480 | tf_op jit(solution)/shard_map/ppermute | solution.py:335
  161.1 28.8 %collective-permute-start.2 = (bf16[576,512]{1,0:T(8,128)(2,1)}, bf16[576,512]{1,0:T(8,128)(2,1)S(1)}, u32[]{:S(2)}, u32[]{:S(2)}) collective-permute-start(bf16[576,512]{1,0:T(8,128)(2,1)} %get-tuple-element.16), channel_id=1, source_target_pairs={{0,4},{1,5},{2,6},{3,7},{4,0},{5,1},{6,2},{7,3},{8,12},{9,13},{10,... | collective-permute-start | bytes 1769480 | tf_op jit(solution)/shard_map/ppermute | solution.py:334
  163.6 26.3 %collective-permute-start.3 = (bf16[576,512]{1,0:T(8,128)(2,1)}, bf16[576,512]{1,0:T(8,128)(2,1)S(1)}, u32[]{:S(2)}, u32[]{:S(2)}) collective-permute-start(bf16[576,512]{1,0:T(8,128)(2,1)} %get-tuple-element.17), channel_id=1, source_target_pairs={{0,6},{1,7},{2,0},{3,1},{4,2},{5,3},{6,4},{7,5},{8,14},{9,15},{10,... | collective-permute-start | bytes 1769480 | tf_op jit(solution)/shard_map/ppermute | solution.py:336
  176.3 13.7 %copy-start.6 = (bf16[576,512]{1,0:T(8,128)(2,1)}, bf16[576,512]{1,0:T(8,128)(2,1)S(1)}, u32[]{:S(2)}) copy-start(bf16[576,512]{1,0:T(8,128)(2,1)S(1)} %collective-permute-done.1.b1) | copy-start | bytes 1769476
  189.9 0.8 copy-start.7
  189.9 1.0 copy-start.8
  189.9 1.3 copy-start.5
  208.0 51.3 %collective-permute-start.5 = (bf16[512,640]{1,0:T(8,128)(2,1)}, bf16[512,640]{1,0:T(8,128)(2,1)S(1)}, u32[]{:S(2)}, u32[]{:S(2)}) collective-permute-start(bf16[512,640]{1,0:T(8,128)(2,1)} %flash.3), channel_id=1, source_target_pairs={{0,4},{1,5},{2,6},{3,7},{4,0},{5,1},{6,2},{7,3},{8,12},{9,13},{10,... | collective-permute-start | bytes 1966088 | tf_op jit(solution)/shard_map/ppermute | solution.py:344
  224.9 34.5 %collective-permute-start.6 = (bf16[512,640]{1,0:T(8,128)(2,1)}, bf16[512,640]{1,0:T(8,128)(2,1)S(1)}, u32[]{:S(2)}, u32[]{:S(2)}) collective-permute-start(bf16[512,640]{1,0:T(8,128)(2,1)} %flash.4), channel_id=1, source_target_pairs={{0,2},{1,3},{2,4},{3,5},{4,6},{5,7},{6,0},{7,1},{8,10},{9,11},{10,... | collective-permute-start | bytes 1966088 | tf_op jit(solution)/shard_map/ppermute | solution.py:344
  241.3 18.1 %collective-permute-start.7 = (bf16[512,640]{1,0:T(8,128)(2,1)}, bf16[512,640]{1,0:T(8,128)(2,1)S(1)}, u32[]{:S(2)}, u32[]{:S(2)}) collective-permute-start(bf16[512,640]{1,0:T(8,128)(2,1)} %flash.5), channel_id=1, source_target_pairs={{0,6},{1,7},{2,0},{3,1},{4,2},{5,3},{6,4},{7,5},{8,14},{9,15},{10,... | collective-permute-start | bytes 1966088 | tf_op jit(solution)/shard_map/ppermute | solution.py:344
  259.3 0.9 copy-start.2
  259.3 1.0 copy-start.3
  259.3 1.2 copy-start.4
